TPU v7x, 512 devices: a whole 4x4x16 slice. The times are simulated.
512 devices in a mesh: dp: 16 (over x_hi, y, core), expert: 32 (over x_lo, z).
Axes of the slice: x: 4 (x_hi: 2, x_lo: 2; x = x_hi * 2 + x_lo), y: 4, z: 16, core: 2. Of those that a mesh axis runs over, the one named last changes fastest.
Arguments:
- tokens: bfloat16 [65536, 1024], P(('dp', 'expert')), may hold values from -6 to 6
- cotangent: bfloat16 [65536, 1024], P(('dp', 'expert')), may hold values from -6 to 6
- picks: int32 [512, 64], P(('dp', 'expert')), may hold values from 0 to 127
- gates: float32 [512, 64], P(('dp', 'expert')), may hold values from 0.1 to 1
- w_gate: bfloat16 [64, 2816, 1024], P('expert', 'dp'), may hold values from -0.1875 to 0.1875
- w_up: bfloat16 [64, 2816, 1024], P('expert', 'dp'), may hold values from -0.1875 to 0.1875
- w_down: bfloat16 [64, 2816, 1024], P('expert', 'dp'), may hold values from -0.109375 to 0.109375
Outputs:
- grad_tokens: bfloat16 [65536, 1024], P(('dp', 'expert'))
- grad_gate: bfloat16 [64, 2816, 1024], P('expert', 'dp')
- grad_up: bfloat16 [64, 2816, 1024], P('expert', 'dp')
- grad_down: bfloat16 [64, 2816, 1024], P('expert', 'dp')
Inputs may be any that keep to these rules, and one draw needn't show every extreme that they name: picks[s, e] is the row, among the 128 tokens of device s, that expert e takes from device s.
All inputs are finite; a program needn't handle non-finite values.
Results may differ from a plain program's by a relative error of at most 0.02.
Values may be sent and summed in bfloat16 or wider, within the bound.
No kernel may reach another device: no remote copies, remote signals or barrier semaphores. Data moves between devices by JAX's collectives and lax.ppermute only.
A program may use at most 64 MiB of HBM per device.

v0:
```python
import jax
import jax.numpy as jnp
from jax import lax
from jax.sharding import PartitionSpec as P


def shards(tokens, cotangent, picks, gates, w_gate, w_up, w_down):
    expert_count = lax.axis_size("expert")
    token_rows, width = tokens.shape
    local_experts = w_gate.shape[0]
    chosen_row = picks[0]
    selector = (chosen_row[:, None] == jnp.arange(token_rows, dtype=jnp.int32)[None, :]).astype(
        jnp.bfloat16
    )
    chosen = jnp.dot(selector, tokens, preferred_element_type=jnp.float32).astype(jnp.bfloat16)
    picked_grad = jnp.dot(selector, cotangent, preferred_element_type=jnp.float32)
    scaled = (picked_grad * gates[0][:, None]).astype(jnp.bfloat16)
    layout = (expert_count, local_experts, width)
    got_x, got_dy = (
        lax.all_to_all(chosen.reshape(layout), "expert", split_axis=0, concat_axis=0, tiled=True),
        lax.all_to_all(scaled.reshape(layout), "expert", split_axis=0, concat_axis=0, tiled=True),
    )
    all_x, all_dy = (
        lax.all_gather(got_x, "dp", axis=0, tiled=True),
        lax.all_gather(got_dy, "dp", axis=0, tiled=True),
    )
    pre_gate = jnp.einsum("sed,efd->esf", all_x, w_gate, preferred_element_type=jnp.float32)
    pre_up = jnp.einsum("sed,efd->esf", all_x, w_up, preferred_element_type=jnp.float32)
    sigmoid_g = jax.nn.sigmoid(pre_gate)
    active = pre_gate * sigmoid_g
    hidden = (active * pre_up).astype(jnp.bfloat16)
    grad_hidden = jnp.einsum("sed,efd->esf", all_dy, w_down, preferred_element_type=jnp.float32)
    grad_down = jnp.einsum(
        "esf,sed->efd", hidden, all_dy, preferred_element_type=jnp.float32
    ).astype(jnp.bfloat16)
    d_up = (grad_hidden * active).astype(jnp.bfloat16)
    d_gate = (grad_hidden * pre_up * sigmoid_g * (1.0 + pre_gate * (1.0 - sigmoid_g))).astype(
        jnp.bfloat16
    )
    grad_gate = jnp.einsum(
        "esf,sed->efd", d_gate, all_x, preferred_element_type=jnp.float32
    ).astype(jnp.bfloat16)
    grad_up = jnp.einsum("esf,sed->efd", d_up, all_x, preferred_element_type=jnp.float32).astype(
        jnp.bfloat16
    )
    first = jnp.einsum("esf,efd->sed", d_gate, w_gate, preferred_element_type=jnp.float32)
    second = jnp.einsum("esf,efd->sed", d_up, w_up, preferred_element_type=jnp.float32)
    summed = lax.psum_scatter(
        (first + second).astype(jnp.bfloat16), "dp", scatter_dimension=0, tiled=True
    ).astype(jnp.float32)
    returned = lax.all_to_all(
        summed.astype(jnp.bfloat16), "expert", split_axis=0, concat_axis=0, tiled=True
    ).astype(summed.dtype)
    back_rows = returned.reshape(expert_count * local_experts, width)
    grad_tokens = jax.ops.segment_sum(back_rows, chosen_row, num_segments=token_rows).astype(
        jnp.bfloat16
    )
    return (grad_tokens, grad_gate, grad_up, grad_down)


def solution(mesh):
    return jax.shard_map(
        shards,
        mesh=mesh,
        in_specs=(
            P(("dp", "expert"), None),
            P(("dp", "expert"), None),
            P(("dp", "expert"), None),
            P(("dp", "expert"), None),
            P("expert", "dp", None),
            P("expert", "dp", None),
            P("expert", "dp", None),
        ),
        out_specs=(
            P(("dp", "expert"), None),
            P("expert", "dp", None),
            P("expert", "dp", None),
            P("expert", "dp", None),
        ),
        check_vma=False,
    )
```

profile of v0, /device:TPU:4, one launch (start us, length us, event | category | flops | bytes accessed | tf_op | source)
XLA Modules:
  0.0 300.1 jit_solution(9503811767197228681)
XLA Ops:
  7.2 0.0 all-gather.5.cloned.1.call-start
  7.2 1.2 convolution_convert_fusion.3
  8.5 0.1 reshape.23
  8.5 32.8 %all_to_all.15 = bf16[32,2,1024]{2,1,0:T(2,128)(2,1)S(1)} all-to-all(bf16[32,2,1024]{2,1,0:T(2,128)(2,1)S(1)} %reshape.23), channel_id=1, replica_groups=mesh['dp'=16,'expert'=32] {'expert'}, dimensions={0} | all-to-all | bytes 262144 | tf_op jit(solution)/shard_map/all_to_all | solution.py:20
  41.3 0.7 copy.17
  42.0 0.0 all-gather.5.cloned.1.call-update
  42.0 0.0 all-gather.3.cloned.1.call-start
  42.1 1.2 fusion.1
  43.2 0.1 reshape.22
  43.3 19.2 %all_to_all.16 = bf16[32,2,1024]{2,1,0:T(2,128)(2,1)S(1)} all-to-all(bf16[32,2,1024]{2,1,0:T(2,128)(2,1)S(1)} %reshape.22), channel_id=1, replica_groups=mesh['dp'=16,'expert'=32] {'expert'}, dimensions={0} | all-to-all | bytes 262144 | tf_op jit(solution)/shard_map/all_to_all | solution.py:21
  62.5 0.7 copy.16
  63.2 0.0 all-gather.3.cloned.1.call-update
  63.2 0.0 reduce-scatter.2.cloned.1.call-start
  63.3 31.0 %all-gather.5.cloned.1.call-done = bf16[512,2,1024]{2,0,1:T(8,128)(2,1)} async-done(((bf16[32,2,1024]{2,0,1:T(8,128)(2,1)}), bf16[512,2,1024]{2,0,1:T(8,128)(2,1)}) %all-gather.5.cloned.1.call-update) | async-done | bytes 2097168 | tf_op jit(solution)/shard_map/all_gather | solution.py:24
  94.3 3.5 %fusion.10 = f32[2,512,176]{1,2,0:T(8,128)} fusion(bf16[512,2,1024]{2,0,1:T(8,128)(2,1)} %all-gather.5.cloned.1.call-done, bf16[2,176,1024]{2,1,0:T(8,128)(2,1)S(1)} %copy-done), kind=kOutput, calls=%fused_computation.21 | convolution fusion | flops 369098752 | bytes 3538944 | tf_op jit(solution)/shard_map/sed,efd->esf/dot_general | solution.py:27
  97.7 1.7 fusion.9
  99.4 60.6 %all-gather.3.cloned.1.call-done = bf16[512,2,1024]{2,0,1:T(8,128)(2,1)} async-done(((bf16[32,2,1024]{2,0,1:T(8,128)(2,1)}), bf16[512,2,1024]{2,0,1:T(8,128)(2,1)}) %all-gather.3.cloned.1.call-update) | async-done | bytes 2097168 | tf_op jit(solution)/shard_map/all_gather | solution.py:25
  160.0 3.1 %multiply_convert_fusion.1 = (bf16[2,512,176]{1,2,0:T(8,128)(2,1)S(1)}, bf16[2,512,176]{1,2,0:T(8,128)(2,1)S(1)}) fusion(f32[2,512,176]{1,2,0:T(8,128)} %fusion.10, f32[2,512,176]{1,2,0:T(8,128)} %fusion.9, bf16[512,2,1024]{2,0,1:T(8,128)(2,1)} %all-gather.3.cloned.1.call-done, bf16[2,176,1024]{2,1,0:T(8,128)(2,1)} %param.13), kind=kOutput, calls=%fused_computation.10 | convolution fusion | flops 371441664 | bytes 4980736 | tf_op jit(solution)/shard_map/sed,efd->esf/dot_general | solution.py:32
  163.2 0.8 fusion.11
  164.0 0.1 copy-done.3
  164.1 2.1 fusion
  166.2 0.0 reduce-scatter.2.cloned.1.call-update
  166.2 1.0 copy-done.4
  167.2 1.4 convolution_convert_fusion.1
  168.6 92.5 %reduce-scatter.2.cloned.1.call-done = bf16[32,2,1024]{2,0,1:T(8,128)(2,1)} async-done(((bf16[512,2,1024]{2,0,1:T(8,128)(2,1)}), bf16[32,2,1024]{2,0,1:T(8,128)(2,1)}) %reduce-scatter.2.cloned.1.call-update) | async-done | bytes 131088 | tf_op jit(solution)/shard_map/reduce_scatter | solution.py:48
  261.0 1.7 copy.18
  262.7 13.2 %all-to-all-start.2 = ((bf16[32,2,1024]{2,1,0:T(2,128)(2,1)}), bf16[32,2,1024]{2,1,0:T(2,128)(2,1)S(1)}, u32[]{:S(2)}, u32[]{:S(2)}) async-start(bf16[32,2,1024]{2,1,0:T(2,128)(2,1)} %copy.18), calls=%async_computation.3 | async-start | bytes 262144 | tf_op jit(solution)/shard_map/all_to_all | solution.py:51
  276.0 1.4 convolution_convert_fusion.2
  277.4 3.1 %convolution_convert_fusion = bf16[2,176,1024]{2,1,0:T(8,128)(2,1)} fusion(bf16[512,2,1024]{2,0,1:T(8,128)(2,1)} %all-gather.3.cloned.1.call-done, f32[2,512,176]{1,2,0:T(8,128)S(1)} %copy-done.8, f32[2,512,176]{1,2,0:T(8,128)S(1)} %copy-done.7), kind=kOutput, calls=%fused_computation.3 | convolution fusion | flops 370540544 | bytes 4259840 | tf_op jit(solution)/shard_map/esf,sed->efd/dot_general | solution.py:33
  280.4 11.0 %all-to-all-done.2 = bf16[32,2,1024]{2,1,0:T(2,128)(2,1)S(1)} async-done(((bf16[32,2,1024]{2,1,0:T(2,128)(2,1)}), bf16[32,2,1024]{2,1,0:T(2,128)(2,1)S(1)}, u32[]{:S(2)}, u32[]{:S(2)}) %all-to-all-start.2) | async-done | bytes 131104 | tf_op jit(solution)/shard_map/all_to_all | solution.py:51
  291.5 1.3 scatter_custom_fusion
  292.8 0.7 convert_element_type.43
  (17 shorter events, 0.1 us)
Async XLA Ops:
  7.2 87.1 %copy-start = (bf16[2,176,1024]{2,1,0:T(8,128)(2,1)S(1)}, bf16[2,176,1024]{2,1,0:T(8,128)(2,1)}, u32[]{:S(2)}) copy-start(bf16[2,176,1024]{2,1,0:T(8,128)(2,1)} %param.11) | copy-start | bytes 2162692
  7.2 87.1 %all-gather.5.cloned.1.call-start = ((), (), s32[]{:S(2)}) async-start(), calls=%async_computation.5 | async-start | bytes 2228224 | tf_op jit(solution)/shard_map/all_gather | solution.py:24
  42.0 118.0 %all-gather.3.cloned.1.call-start = ((), (), s32[]{:S(2)}) async-start(), calls=%async_computation.4 | async-start | bytes 2228224 | tf_op jit(solution)/shard_map/all_gather | solution.py:25
  43.3 54.4 %copy-start.2 = (bf16[2,176,1024]{2,1,0:T(8,128)(2,1)S(1)}, bf16[2,176,1024]{2,1,0:T(8,128)(2,1)}, u32[]{:S(2)}) copy-start(bf16[2,176,1024]{2,1,0:T(8,128)(2,1)} %param.12) | copy-start | bytes 2162692
  63.2 197.8 %reduce-scatter.2.cloned.1.call-start = ((), (), s32[]{:S(2)}) async-start(), calls=%async_computation.6 | async-start | bytes 2228224 | tf_op jit(solution)/shard_map/reduce_scatter | solution.py:48
  94.3 3.5 %copy-start.1 = (bf16[512,2,1024]{2,0,1:T(8,128)(2,1)S(1)}, bf16[512,2,1024]{2,0,1:T(8,128)(2,1)}, u32[]{:S(2)}) copy-start(bf16[512,2,1024]{2,0,1:T(8,128)(2,1)} %all-gather.5.cloned.1.call-done) | copy-start | bytes 6291460
  163.2 0.8 copy-start.5
  163.2 0.8 copy-start.3
  166.2 1.0 copy-start.4
  167.2 108.8 %copy-start.6 = (bf16[2,512,176]{1,2,0:T(8,128)(2,1)S(1)}, bf16[2,512,176]{1,2,0:T(8,128)(2,1)}, u32[]{:S(2)}) copy-start(bf16[2,512,176]{1,2,0:T(8,128)(2,1)} %copy-done.5) | copy-start | bytes 1081348
  262.7 28.7 %all-to-all-start.2 = ((bf16[32,2,1024]{2,1,0:T(2,128)(2,1)}), bf16[32,2,1024]{2,1,0:T(2,128)(2,1)S(1)}, u32[]{:S(2)}, u32[]{:S(2)}) async-start(bf16[32,2,1024]{2,1,0:T(2,128)(2,1)} %copy.18), calls=%async_computation.3 | async-start | bytes 262144 | tf_op jit(solution)/shard_map/all_to_all | solution.py:51
  275.9 1.4 copy-start.7
  275.9 1.4 copy-start.8
Sparse Core Ops, SparseCore 0:
  42.1 52.0 all-gather.4
  98.2 61.7 all-gather.2
  166.3 94.6 reduce-scatter.1
where the time goes:
time: 300 us
  waiting for transfers between devices  195 us (65%)
  blocking collectives  52 us (17%)
  matrix products  19.5 us (6%)
  between operations  13.9 us (5%)
  starting transfers between devices  13.3 us (4%)
  local copies, waits for them, and re-layouts  4.26 us (1%)
    reduce_scatter x1, waiting for transfers between devices, shards(): lax.psum_scatter((first + second).astype(jnp.bfloat16), 'dp', scatter_dim...  92.5 us
    all_gather x1, waiting for transfers between devices, shards(): lax.all_gather(got_dy, 'dp', axis=0, tiled=True)  60.6 us
    all_to_all x1, blocking collectives, shards(): lax.all_to_all(chosen.reshape(layout), 'expert', split_axis=0, concat_axi...  32.8 us
    all_gather x1, waiting for transfers between devices, shards(): lax.all_gather(got_x, 'dp', axis=0, tiled=True)  31 us
    all_to_all x1, blocking collectives, shards(): lax.all_to_all(scaled.reshape(layout), 'expert', split_axis=0, concat_axi...  19.2 us
    all_to_all x1, starting transfers between devices, shards(): lax.all_to_all(summed.astype(jnp.bfloat16), 'expert', split_axis=0, conca...  13.2 us
    all_to_all x1, waiting for transfers between devices, shards(): lax.all_to_all(summed.astype(jnp.bfloat16), 'expert', split_axis=0, conca...  11 us
  transfers between devices with their start and end apart: 4, of which 4 were waited for; matrix products, arithmetic and copies ran while one was open for 4% of the time, Pallas kernels for 0%

commit v1 on v0

--- a/solution.py
+++ b/solution.py
@@ -22,7 +22,15 @@
     )
     all_x, all_dy = (
         lax.all_gather(got_x, "dp", axis=0, tiled=True),
-        lax.all_gather(got_dy, "dp", axis=0, tiled=True),
+        jnp.concatenate(
+            lax.all_to_all(
+                jnp.stack([got_dy] * lax.axis_size("dp")),
+                axis_name="dp",
+                split_axis=0,
+                concat_axis=0,
+            ),
+            axis=0,
+        ),
     )
     pre_gate = jnp.einsum("sed,efd->esf", all_x, w_gate, preferred_element_type=jnp.float32)
     pre_up = jnp.einsum("sed,efd->esf", all_x, w_up, preferred_element_type=jnp.float32)

time: 300 us -> 241 us (0.80)
  waiting for transfers between devices: 195 us -> 97.1 us
  blocking collectives: 52 us -> 91 us
  matrix products: 19.5 us -> 15.2 us
  local copies, waits for them, and re-layouts: 4.26 us -> 7.3 us
    all_gather x1 -> x0, waiting for transfers between devices: 60.6 us -> none  [shards(): lax.all_gather(got_dy, 'dp', axis=0, tiled=True)]
    all_to_all x0 -> x1, blocking collectives: none -> 39.2 us  [shards(): lax.all_to_all(jnp.stack([got_dy] * lax.axis_size('dp')), axis_name='dp',...]
    all_gather x1, waiting for transfers between devices: 31 us -> 0.01 us  [shards(): lax.all_gather(got_x, 'dp', axis=0, tiled=True)]
    reduce_scatter x1, waiting for transfers between devices: 92.5 us -> 86.2 us  [shards(): lax.psum_scatter((first + second).astype(jnp.bfloat16), 'dp', scatter_dim...]
  transfers between devices with their start and end apart: 4 -> 3, of which waited for: 4 -> 2; matrix products, arithmetic and copies ran while one was open for 4% -> 4% of each run, Pallas kernels for 0% -> 0%
where the time goes in v1:
time: 241 us; the launch traced here: 240 us
  waiting for transfers between devices  97.1 us (40%)
  blocking collectives  91 us (38%)
  matrix products  15.2 us (6%)
  between operations  14.2 us (6%)
  starting transfers between devices  13.3 us (6%)
  local copies, waits for them, and re-layouts  7.3 us (3%)
    reduce_scatter x1, waiting for transfers between devices, shards(): lax.psum_scatter((first + second).astype(jnp.bfloat16), 'dp', scatter_dim...  86.2 us
    all_to_all x1, blocking collectives, shards(): lax.all_to_all(jnp.stack([got_dy] * lax.axis_size('dp')), axis_name='dp',...  39.2 us
    all_to_all x1, blocking collectives, shards(): lax.all_to_all(chosen.reshape(layout), 'expert', split_axis=0, concat_axi...  32.8 us
    all_to_all x1, blocking collectives, shards(): lax.all_to_all(scaled.reshape(layout), 'expert', split_axis=0, concat_axi...  19.1 us
    all_to_all x1, starting transfers between devices, shards(): lax.all_to_all(summed.astype(jnp.bfloat16), 'expert', split_axis=0, conca...  13.2 us
    all_to_all x1, waiting for transfers between devices, shards(): lax.all_to_all(summed.astype(jnp.bfloat16), 'expert', split_axis=0, conca...  10.9 us
  transfers between devices with their start and end apart: 3, of which 2 were waited for; matrix products, arithmetic and copies ran while one was open for 4% of the time, Pallas kernels for 0%

profile of v1, /device:TPU:4, one launch (start us, length us, event | category | flops | bytes accessed | tf_op | source)
XLA Modules:
  0.0 240.3 jit_solution(15167621988703329014)
XLA Ops:
  7.2 0.0 all-gather.2.cloned.1.call-start
  7.2 1.2 convolution_convert_fusion.3
  8.5 0.1 reshape.29
  8.5 32.8 %all_to_all.20 = bf16[32,2,1024]{2,1,0:T(2,128)(2,1)S(1)} all-to-all(bf16[32,2,1024]{2,1,0:T(2,128)(2,1)S(1)} %reshape.29), channel_id=1, replica_groups=mesh['dp'=16,'expert'=32] {'expert'}, dimensions={0} | all-to-all | bytes 262144 | tf_op jit(solution)/shard_map/all_to_all | solution.py:20
  41.3 0.7 copy.18
  42.0 0.0 reduce-scatter.2.cloned.1.call-start
  42.1 1.2 fusion.1
  43.2 0.1 reshape.27
  43.3 19.1 %all_to_all.21 = bf16[32,2,1024]{2,1,0:T(2,128)(2,1)S(1)} all-to-all(bf16[32,2,1024]{2,1,0:T(2,128)(2,1)S(1)} %reshape.27), channel_id=1, replica_groups=mesh['dp'=16,'expert'=32] {'expert'}, dimensions={0} | all-to-all | bytes 262144 | tf_op jit(solution)/shard_map/all_to_all | solution.py:21
  62.4 0.2 stack.2
  62.7 39.2 %all_to_all.22 = bf16[16,32,2,1024]{3,1,2,0:T(8,128)(2,1)S(1)} all-to-all(bf16[16,32,2,1024]{3,1,2,0:T(8,128)(2,1)S(1)} %stack.2), channel_id=1, replica_groups=mesh['dp'=16,'expert'=32] {'dp'}, dimensions={0} | all-to-all | bytes 4194304 | tf_op jit(solution)/shard_map/all_to_all | solution.py:26
  101.9 1.5 copy.17
  103.4 2.6 %fusion.10 = f32[2,512,176]{1,2,0:T(8,128)S(1)} fusion(bf16[512,2,1024]{2,0,1:T(8,128)(2,1)} %all-gather.2.cloned.1.call-done, bf16[2,176,1024]{2,1,0:T(8,128)(2,1)S(1)} %copy-done), kind=kOutput, calls=%fused_computation.21 | convolution fusion | flops 369098752 | bytes 3538944 | tf_op jit(solution)/shard_map/sed,efd->esf/dot_general | solution.py:35
  106.0 0.8 fusion.9
  106.9 1.0 copy-done.3
  107.9 0.4 copy-done.12
  108.3 1.0 multiply_convert_fusion.1
  109.3 0.8 fusion.11
  110.1 0.1 copy-done.5
  110.2 2.1 fusion
  112.3 1.0 copy-done.6
  113.3 1.4 convolution_convert_fusion.1
  114.7 86.2 %reduce-scatter.2.cloned.1.call-done = bf16[32,2,1024]{2,0,1:T(8,128)(2,1)} async-done(((bf16[512,2,1024]{2,0,1:T(8,128)(2,1)}), bf16[32,2,1024]{2,0,1:T(8,128)(2,1)}) %reduce-scatter.2.cloned.1.call-update) | async-done | bytes 131088 | tf_op jit(solution)/shard_map/reduce_scatter | solution.py:56
  200.9 1.7 copy.19
  202.6 13.2 %all-to-all-start.3 = ((bf16[32,2,1024]{2,1,0:T(2,128)(2,1)}), bf16[32,2,1024]{2,1,0:T(2,128)(2,1)S(1)}, u32[]{:S(2)}, u32[]{:S(2)}) async-start(bf16[32,2,1024]{2,1,0:T(2,128)(2,1)} %copy.19), calls=%async_computation.4 | async-start | bytes 262144 | tf_op jit(solution)/shard_map/all_to_all | solution.py:59
  215.8 1.4 convolution_convert_fusion.2
  217.2 0.3 copy-done.4
  217.5 0.3 copy-done.10
  217.8 2.6 %convolution_convert_fusion = bf16[2,176,1024]{2,1,0:T(8,128)(2,1)} fusion(bf16[512,2,1024]{2,0,1:T(8,128)(2,1)S(1)} %bitcast.23, f32[2,512,176]{1,2,0:T(8,128)} %copy-done.11, f32[2,512,176]{1,2,0:T(8,128)S(1)} %copy-done.10), kind=kOutput, calls=%fused_computation.3 | convolution fusion | flops 370540544 | bytes 4259840 | tf_op jit(solution)/shard_map/esf,sed->efd/dot_general | solution.py:41
  220.4 10.9 %all-to-all-done.3 = bf16[32,2,1024]{2,1,0:T(2,128)(2,1)S(1)} async-done(((bf16[32,2,1024]{2,1,0:T(2,128)(2,1)}), bf16[32,2,1024]{2,1,0:T(2,128)(2,1)S(1)}, u32[]{:S(2)}, u32[]{:S(2)}) %all-to-all-start.3) | async-done | bytes 131104 | tf_op jit(solution)/shard_map/all_to_all | solution.py:59
  231.3 1.3 scatter_custom_fusion
  232.7 0.7 convert_element_type.43
  (25 shorter events, 0.2 us)
Async XLA Ops:
  7.2 96.2 %copy-start = (bf16[2,176,1024]{2,1,0:T(8,128)(2,1)S(1)}, bf16[2,176,1024]{2,1,0:T(8,128)(2,1)}, u32[]{:S(2)}) copy-start(bf16[2,176,1024]{2,1,0:T(8,128)(2,1)} %param.11) | copy-start | bytes 2162692
  7.2 96.2 %all-gather.2.cloned.1.call-start = ((), (), s32[]{:S(2)}) async-start(), calls=%async_computation.5 | async-start | bytes 2228224 | tf_op jit(solution)/shard_map/all_gather | solution.py:24
  42.0 158.9 %reduce-scatter.2.cloned.1.call-start = ((), (), s32[]{:S(2)}) async-start(), calls=%async_computation.6 | async-start | bytes 2228224 | tf_op jit(solution)/shard_map/reduce_scatter | solution.py:56
  103.4 2.6 %copy-start.2 = (bf16[2,176,1024]{2,1,0:T(8,128)(2,1)S(1)}, bf16[2,176,1024]{2,1,0:T(8,128)(2,1)}, u32[]{:S(2)}) copy-start(bf16[2,176,1024]{2,1,0:T(8,128)(2,1)} %param.12) | copy-start | bytes 2162692
  103.4 2.6 %copy-start.1 = (bf16[512,2,1024]{2,0,1:T(8,128)(2,1)S(1)}, bf16[512,2,1024]{2,0,1:T(8,128)(2,1)}, u32[]{:S(2)}) copy-start(bf16[512,2,1024]{2,0,1:T(8,128)(2,1)} %all-gather.2.cloned.1.call-done) | copy-start | bytes 6291460
  106.0 3.3 %copy-start.9 = (f32[2,512,176]{1,2,0:T(8,128)}, f32[2,512,176]{1,2,0:T(8,128)S(1)}, u32[]{:S(2)}) copy-start(f32[2,512,176]{1,2,0:T(8,128)S(1)} %fusion.10) | copy-start | bytes 2162692
  106.0 1.9 copy-start.3
  106.0 2.3 copy-start.12
  106.9 2.4 %copy-start.11 = (f32[2,512,176]{1,2,0:T(8,128)}, f32[2,512,176]{1,2,0:T(8,128)S(1)}, u32[]{:S(2)}) copy-start(f32[2,512,176]{1,2,0:T(8,128)S(1)} %fusion.9) | copy-start | bytes 2162692
  109.3 0.8 copy-start.7
  109.3 0.8 copy-start.5
  112.3 1.0 copy-start.6
  113.3 102.5 %copy-start.8 = (bf16[2,512,176]{1,2,0:T(8,128)(2,1)S(1)}, bf16[2,512,176]{1,2,0:T(8,128)(2,1)}, u32[]{:S(2)}) copy-start(bf16[2,512,176]{1,2,0:T(8,128)(2,1)} %copy-done.7) | copy-start | bytes 1081348
  202.6 28.7 %all-to-all-start.3 = ((bf16[32,2,1024]{2,1,0:T(2,128)(2,1)}), bf16[32,2,1024]{2,1,0:T(2,128)(2,1)S(1)}, u32[]{:S(2)}, u32[]{:S(2)}) async-start(bf16[32,2,1024]{2,1,0:T(2,128)(2,1)} %copy.19), calls=%async_computation.4 | async-start | bytes 262144 | tf_op jit(solution)/shard_map/all_to_all | solution.py:59
  215.8 1.7 copy-start.4
  215.8 2.0 copy-start.10
Sparse Core Ops, SparseCore 0:
  42.1 60.2 all-gather.1
  112.5 88.4 reduce-scatter.1
